TPU v7x, 256 devices: a whole 4x4x8 slice. The times are simulated.
256 devices in a mesh: ctx: 64 (over z, y, core), head: 4 (over x).
Axes of the slice: x: 4, y: 4, z: 8, core: 2. Of those that a mesh axis runs over, the one named last changes fastest.
Arguments:
- queries: bfloat16 [16384, 2560], P('ctx', 'head'), may hold values from -90 to 90
- keys: bfloat16 [16384, 512], P('ctx', 'head'), may hold values from -4.5 to 4.5
- block_position: int32 [256], P('ctx'), may hold values from 0 to 255, as said below
- w_gate_q: bfloat16 [4, 640, 128], P('head'), may hold values from -0.25 to 0.25
- w_gate_k: bfloat16 [4, 384, 128], P('head'), may hold values from -0.3125 to 0.3125
Outputs:
- target_map: float32 [256, 4, 256], P('ctx', 'head')
- grad_gate_q: float32 [4, 640, 128], P('head')
- grad_gate_k: float32 [4, 384, 128], P('head')
- mean_loss: float32 [], replicated
Inputs may be any that keep to these rules, and one draw needn't show every extreme that they name: `block_position`: each index of ctx holds 4 blocks that lie one after the other in the sequence, in increasing order; the 256 entries name every block once. The runs of indices i and i + 32 of ctx are mirrored: their run numbers (first block divided by 4) add to 63.
All inputs are finite; a program needn't handle non-finite values.
Results may differ from a plain program's by a relative error of at most 0.0038.
The roundings to bfloat16 on the way count: a program that leaves them out, or rounds other values in their place, can miss the bound.
Values may be sent and summed in bfloat16 or wider, within the bound.
A program may use at most 64 MiB of HBM per device.

v0:
```python
import math

import jax
import jax.numpy as jnp
from jax import lax
from jax.sharding import PartitionSpec as P

BLK = 64


MASKED_SCORE = -1e30


def expand_positions(block_starts):
    offsets = jnp.arange(BLK, dtype=jnp.int32)
    return (block_starts[:, None] * BLK + offsets[None, :]).reshape(-1)


def by_shard(update, tok_dev, running, shard_keys):
    shard_count = shard_keys.shape[0] // tok_dev

    def fold_one(shard_step, state):
        one_shard = lax.dynamic_slice_in_dim(shard_keys, shard_step * tok_dev, tok_dev)
        return update(state, one_shard, shard_step * tok_dev)

    return lax.fori_loop(0, shard_count, fold_one, running)


def per_device(queries, keys, block_position, w_gate_q, w_gate_k):
    tok_dev, query_width = queries.shape
    head_dim = keys.shape[1]
    group_size = query_width // head_dim
    blk_dev = tok_dev // BLK
    score_scale = 1.0 / math.sqrt(head_dim)
    block_table = lax.all_gather(block_position, "ctx", axis=0, tiled=True)
    nblk = block_table.shape[0]
    own_pos = expand_positions(block_position)
    row_ranges = [(0, tok_dev)]
    query_heads = queries.reshape(tok_dev, group_size, head_dim)
    row_shape = (group_size, tok_dev)

    def shard_scores(one_shard, first_row):
        key_pos = expand_positions(lax.dynamic_slice_in_dim(block_table, first_row // BLK, blk_dev))
        scores = (
            jnp.einsum("rgd,nd->grn", query_heads, one_shard, preferred_element_type=jnp.float32)
            * score_scale
        )
        allowed = key_pos[None, None, :] <= own_pos[None, :, None]
        return jnp.where(allowed, scores, MASKED_SCORE)

    def is_future(first_row):
        key_blocks = lax.dynamic_slice_in_dim(block_table, first_row // BLK, blk_dev)
        return jnp.min(key_blocks) * BLK > jnp.max(own_pos)

    def keep_state(state):
        return state

    def stats_update(running, one_shard, first_row):
        row_top, row_total = running
        row_start, row_stop = row_ranges[0]

        def stats_refresh(state, row_start=row_start, row_stop=row_stop):
            old_top, old_total = state
            scores = shard_scores(one_shard, first_row)
            new_top = jnp.maximum(old_top, jnp.max(scores, axis=2))
            new_total = old_total * jnp.exp(old_top - new_top) + jnp.sum(
                jnp.exp(scores - new_top[:, :, None]), axis=2
            )
            return (new_top, new_total)

        part_state = (row_top, row_total)
        new_top, new_total = lax.cond(is_future(first_row), keep_state, stats_refresh, part_state)
        return (new_top, new_total)

    start_stats = (
        jnp.full(row_shape, MASKED_SCORE, jnp.float32),
        jnp.zeros(row_shape, jnp.float32),
    )
    row_top, row_total = by_shard(
        stats_update, tok_dev, start_stats, lax.all_gather(keys, "ctx", axis=0, tiled=True)
    )

    def pool_update(running, one_shard, first_row):
        row_start, row_stop = row_ranges[0]

        def pool_refresh(state, row_start=row_start, row_stop=row_stop):
            scores = shard_scores(one_shard, first_row)
            probs = (
                jnp.exp(scores - row_top[:, row_start:row_stop, None])
                / row_total[:, row_start:row_stop, None]
            )
            block_max = jnp.max(
                probs.reshape(group_size, row_stop - row_start, blk_dev, BLK), axis=(0, 3)
            )
            return lax.dynamic_update_slice_in_dim(state, block_max, first_row // BLK, 1)

        new_part = lax.cond(is_future(first_row), keep_state, pool_refresh, running)
        return new_part

    start_pool = jnp.zeros((tok_dev, nblk), jnp.float32)
    row_blocks = by_shard(
        pool_update, tok_dev, start_pool, lax.all_gather(keys, "ctx", axis=0, tiled=True)
    )
    pooled = jnp.max(row_blocks.reshape(blk_dev, BLK, nblk), axis=1)
    block_target = pooled / jnp.sum(pooled, axis=1, keepdims=True)
    to_global = (block_table[:, None] == jnp.arange(nblk, dtype=jnp.int32)[None, :]).astype(
        jnp.float32
    )
    target_map = jnp.dot(block_target, to_global, precision=lax.Precision.HIGHEST)[:, None, :]
    pooled_query = jnp.mean(
        queries.astype(jnp.float32).reshape(blk_dev, BLK, query_width), axis=1
    ).astype(jnp.bfloat16)
    key_float = keys.astype(jnp.float32).reshape(blk_dev, BLK, head_dim)
    key_features = jnp.concatenate(
        [jnp.max(key_float, axis=1), jnp.min(key_float, axis=1), jnp.mean(key_float, axis=1)],
        axis=1,
    ).astype(jnp.bfloat16)
    gate_query = jnp.dot(pooled_query, w_gate_q[0], preferred_element_type=jnp.float32).astype(
        jnp.bfloat16
    )
    query_float = gate_query.astype(jnp.float32)
    gate_key = jnp.dot(key_features, w_gate_k[0], preferred_element_type=jnp.float32).astype(
        jnp.bfloat16
    )
    all_keys = lax.all_gather(gate_key, "ctx", axis=0, tiled=True)
    allowed = block_table[None, :] <= block_position[:, None]
    logits = jnp.dot(gate_query, all_keys.T, preferred_element_type=jnp.float32) * score_scale
    logits = jnp.where(allowed, logits, MASKED_SCORE)
    logit_top = jnp.max(logits, axis=1, keepdims=True)
    log_prob = (
        logits - logit_top - jnp.log(jnp.sum(jnp.exp(logits - logit_top), axis=1, keepdims=True))
    )
    gate_prob = jnp.exp(log_prob)
    loss_part = -jnp.sum(jnp.where(allowed, block_target * log_prob, 0.0))
    delta = gate_prob - block_target
    query_delta = (
        jnp.dot(delta, all_keys.astype(jnp.float32), precision=lax.Precision.HIGHEST) * score_scale
    )
    grad_query = jnp.dot(
        pooled_query.astype(jnp.float32).T, query_delta, precision=lax.Precision.HIGHEST
    )
    key_terms = jnp.dot(delta.T, query_float, precision=lax.Precision.HIGHEST) * score_scale
    key_delta = lax.psum_scatter(key_terms, "ctx", scatter_dimension=0, tiled=True)
    grad_key = jnp.dot(
        key_features.astype(jnp.float32).T, key_delta, precision=lax.Precision.HIGHEST
    )
    grad_query, grad_key, loss_cycle = lax.psum((grad_query, grad_key, loss_part), "ctx")
    loss_all = lax.psum(loss_cycle, "head")
    mean_loss = loss_all / (nblk * lax.axis_size("head"))
    return (target_map, grad_query[None], grad_key[None], mean_loss)


def solution(mesh):
    return jax.shard_map(
        per_device,
        mesh=mesh,
        in_specs=(
            P("ctx", "head"),
            P("ctx", "head"),
            P("ctx"),
            P("head", None, None),
            P("head", None, None),
        ),
        out_specs=(P("ctx", "head", None), P("head", None, None), P("head", None, None), P()),
        check_vma=False,
    )
```

profile of v0, /device:TPU:1, one launch (start us, length us, event | category | flops | bytes accessed | tf_op | source)
XLA Modules:
  0.0 985.9 jit_solution(10263843384814325698)
XLA Ops:
  10.9 20.8 %all-reduce = s32[256]{0:T(256)S(1)} all-reduce(s32[256]{0:T(256)S(1)} %dynamic-update-slice), channel_id=1, replica_groups=mesh['ctx'=64,'head'=4] {'ctx'}, use_global_device_ids=true, to_apply=%add | all-reduce | flops 256 | bytes 2048
  31.9 46.0 %all-gather = bf16[64,4,128]{2,1,0:T(4,128)(2,1)S(1)} all-gather(bf16[1,4,128]{2,1,0:T(4,128)(2,1)S(1)} %fusion.19), channel_id=1, replica_groups=mesh['ctx'=64,'head'=4] {'ctx'}, dimensions={0}, use_global_device_ids=true | all-gather | bytes 66560 | tf_op jit(solution)/shard_map/all_gather | solution.py:125
  80.0 14.2 %all-gather.3.cloned.1.call-done = bf16[16384,128]{1,0:T(8,128)(2,1)} async-done(((bf16[256,128]{1,0:T(8,128)(2,1)}), bf16[16384,128]{1,0:T(8,128)(2,1)}) %all-gather.3.cloned.1.call-update) | async-done | bytes 4194320 | tf_op jit(solution)/shard_map/all_gather | solution.py:102
  94.1 183.7 %while.37 = (s32[]{:T(128)}, f32[5,256]{1,0:T(8,128)S(1)}, f32[5,256]{1,0:T(8,128)S(1)}, s32[256]{0:T(256)S(1)}, s32[]{:T(128)}, /*index=5*/bf16[16384,128]{1,0:...) while((s32[]{:T(128)}, f32[5,256]{1,0:T(8,128)S(1)}, ...), condition=%wide.region_7.8_spmd.clone, body=%wide.region_1.7_spmd.clone.sunk | while | flops 85593136 | bytes 3223300 | solution.py:26
  277.9 185.1 %while.38 = (s32[]{:T(128)}, f32[256,256]{0,1:T(8,128)S(1)}, s32[256]{0:T(256)S(1)}, s32[]{:T(128)}, bf16[16384,128]{1,0:T(8,128)(2,1)}, /*index=5*/bf16[256,5,1...) while((s32[]{:T(128)}, f32[256,256]{0,1:T(8,128)S(1)}, ...), condition=%wide.region_14.15_spmd.clone, body=%wide.region_8.14_spmd.clone.sunk | while | flops 85589552 | bytes 1082112 | solution.py:26
  282.0 2.1 conditional.7
  298.6 2.1 conditional.7
  311.1 2.1 conditional.7
  325.6 2.1 conditional.7
  338.0 2.1 conditional.7
  346.4 2.1 conditional.7
  350.6 2.1 conditional.7
  363.1 2.1 conditional.7
  379.8 2.2 conditional.7
  388.1 2.1 conditional.7
  398.5 2.1 conditional.7
  417.2 2.1 conditional.7
  421.4 2.1 conditional.7
  425.6 2.1 conditional.7
  440.2 2.1 conditional.7
  465.7 327.4 %all-reduce.6.cloned.1.call-done = f32[256,128]{1,0:T(8,128)} async-done(((f32[256,128]{1,0:T(8,128)}), f32[256,128]{1,0:T(8,128)}) %all-reduce.6.cloned.1.call-update) | async-done | bytes 131088
  796.1 123.1 %psum.30 = f32[]{:T(128)} all-reduce(f32[]{:T(128)S(6)} %neg.3), channel_id=1, replica_groups=mesh['ctx'=64,'head'=4] {'ctx'}, use_global_device_ids=true, to_apply=%region_27.28 | all-reduce | flops 1 | bytes 8 | tf_op jit(solution)/shard_map/psum | solution.py:147
  919.3 9.0 psum.31
  929.8 45.1 %all-reduce.8.cloned.1.call-done = (f32[1,640,128]{2,1,0:T(8,128)}, f32[1,384,128]{2,1,0:T(8,128)}) async-done(((f32[1,640,128]{2,1,0:T(8,128)}, f32[1,384,128]{2,1,0:T(8,128)}), (f32[1,640,128]{2,1,0:T(8,128)}, f32[1,384,128]{2,1,0:T(8,128)})) %all-reduce.8.cloned.1.call-update) | async-done | bytes 524304 | tf_op jit(solution)/shard_map/psum | solution.py:147
  (996 shorter events, 279.5 us)
Async XLA Ops:
  7.2 70.8 %copy-start = (bf16[1,640,128]{2,1,0:T(8,128)(2,1)S(1)}, bf16[1,640,128]{2,1,0:T(8,128)(2,1)}, u32[]{:S(2)}) copy-start(bf16[1,640,128]{2,1,0:T(8,128)(2,1)} %param.16) | copy-start | bytes 491524
  7.2 2.2 copy-start.4
  7.2 24.5 %copy-start.2 = (bf16[256,128]{1,0:T(8,128)(2,1)S(1)}, bf16[256,128]{1,0:T(8,128)(2,1)}, u32[]{:S(2)}) copy-start(bf16[256,128]{1,0:T(8,128)(2,1)} %param.14) | copy-start | bytes 196612
  7.2 70.7 %copy-start.1 = (bf16[256,640]{1,0:T(8,128)(2,1)S(1)}, bf16[256,640]{1,0:T(8,128)(2,1)}, u32[]{:S(2)}) copy-start(bf16[256,640]{1,0:T(8,128)(2,1)} %param.13) | copy-start | bytes 983044
  7.2 3.5 copy-start.5
  7.2 24.5 %copy-start.3 = (bf16[1,384,128]{2,1,0:T(8,128)(2,1)S(1)}, bf16[1,384,128]{2,1,0:T(8,128)(2,1)}, u32[]{:S(2)}) copy-start(bf16[1,384,128]{2,1,0:T(8,128)(2,1)} %param.17) | copy-start | bytes 294916
  7.2 86.9 %all-gather.3.cloned.1.call-start = ((), (), s32[]{:S(2)}) async-start(), calls=%async_computation | async-start | bytes 4259840 | tf_op jit(solution)/shard_map/all_gather | solution.py:102
  8.0 785.1 %all-reduce.6.cloned.1.call-start = ((), (), s32[]{:S(2)}) async-start(), calls=%async_computation.1 | async-start | bytes 262144
  464.6 510.3 %all-reduce.8.cloned.1.call-start = ((), (), s32[]{:S(2)}) async-start(), calls=%async_computation.2 | async-start | bytes 1048576 | tf_op jit(solution)/shard_map/psum | solution.py:147
Sparse Core Ops, SparseCore 0:
  10.8 83.2 all-gather.2
  464.7 328.3 all-reduce.5
  797.2 177.6 all-reduce.7
where the time goes:
time: 995 us; the launch traced here: 986 us
  waiting for transfers between devices  387 us (39%)
  blocking collectives  199 us (20%)
  loops' own time  176 us (18%)
  other arithmetic  117 us (12%)
  matrix products  69.2 us (7%)
  local copies, waits for them, and re-layouts  19.3 us (2%)
  between operations  17.7 us (2%)
    unnamed x4, waiting for transfers between devices  328 us
    another operation x2, loops' own time, by_shard(): return lax.fori_loop(0, shard_count, fold_one, running)  170 us
    psum x1, blocking collectives, per_device(): lax.psum((grad_query, grad_key, loss_part), 'ctx')  123 us
    reduce_min x128, other arithmetic, is_future(): return jnp.min(key_blocks) * BLK > jnp.max(own_pos)  92.8 us
    dot_general x50, matrix products, shard_scores(): jnp.einsum('rgd,nd->grn', query_heads, one_shard, preferred_element_type=...  64.5 us
    all_gather x1, blocking collectives, per_device(): all_keys = lax.all_gather(gate_key, 'ctx', axis=0, tiled=True)  46 us
    psum x1, waiting for transfers between devices, per_device(): lax.psum((grad_query, grad_key, loss_part), 'ctx')  45.1 us
    unnamed x1, blocking collectives  20.8 us
  transfers between devices with their start and end apart: 3, of which 3 were waited for; matrix products, arithmetic and copies ran while one was open for 1% of the time, Pallas kernels for 0%

commit v1 on v0

v1 whole, which is shorter than its diff:
```python
import functools
import math

import jax
import jax.numpy as jnp
from jax import lax
from jax.experimental import pallas as pl
from jax.experimental.pallas import tpu as pltpu
from jax.sharding import PartitionSpec as P

ZS, YS, XS = 8, 4, 4
BLK, HD, GQ = 64, 128, 5
TOK = 256
HALF = 128
ROWS = HALF + 16
NEG = -1e30
LOG2E = 1.4426950408889634
SCALE = 1.0 / math.sqrt(HD)
F32, BF16 = jnp.float32, jnp.bfloat16
MESH = pl.DeviceIdType.MESH


def nt(a, b):
    return lax.dot_general(a, b, (((1,), (1,)), ((), ())), preferred_element_type=F32)


def tn(a, b):
    return lax.dot_general(a, b, (((0,), (0,)), ((), ())), preferred_element_type=F32)


def mm(a, b):
    return jnp.dot(a, b, preferred_element_type=F32)


def split2(a):
    hi = a.astype(BF16)
    return hi, (a - hi.astype(F32)).astype(BF16)


def split3(a):
    hi, mid = split2(a)
    return hi, mid, (a - hi.astype(F32) - mid.astype(F32)).astype(BF16)


def iota(shape, dim):
    return lax.broadcasted_iota(jnp.int32, shape, dim)


def kernel(
    q_ref, k_ref, pos_ref, wq_ref, wk_ref,
    map_ref, gq_ref, gk_ref, loss_ref,
    k0, k1, qt, bm8, bmd, m8, l8, posv, kfb, pqb, posi, posii, u8, tb, lx,
    s_y0, s_z0, s_s0, s_z1, s_y1, s_s1, s_t, s_ts, s_x,
    r_y0, r_z0, r_s0, r_z1, r_y1, r_s1, r_t, r_ts, r_x,
):
    ctx, x = lax.axis_index("ctx"), lax.axis_index("head")
    c = lax.rem(ctx, 2)
    y = lax.rem(ctx // 2, YS)
    z = ctx // (2 * YS)

    def zz(d):
        return lax.rem(z + (d + ZS), ZS)

    def yy(d):
        return lax.rem(y + d, YS)

    def dev(z_at, y_at, c_at):
        return ((z_at * YS + y_at) * 2 + c_at, x)

    up, down, sib = dev(zz(1), y, c), dev(zz(-1), y, c), dev(z, y, 1 - c)
    y_peers = [dev(z, yy(d), c) for d in (1, 2, 3)]
    x_peers = [(ctx, lax.rem(x + d, XS)) for d in (1, 2, 3)]

    barrier = pltpu.get_barrier_semaphore()
    peers = [up, down, sib] + y_peers + x_peers
    for peer in peers:
        pl.semaphore_signal(barrier, inc=1, device_id=peer, device_id_type=MESH)

    def send(src, dst, s_sem, r_sem, to):
        pltpu.make_async_remote_copy(
            src_ref=src, dst_ref=dst, send_sem=s_sem, recv_sem=r_sem,
            device_id=to, device_id_type=MESH,
        ).start()

    def wait(like, sem):
        pltpu.make_async_copy(like, like, sem).wait()

    first = pos_ref[0].astype(F32)
    row16 = iota((16, TOK), 0)
    tok16 = iota((16, TOK), 1)
    for half, buf in ((0, k0), (1, k1)):
        pooled = jnp.zeros((16, HD), F32)
        for g in range(GQ):
            pick = (row16 // 2 == g) & (tok16 // BLK == half * 2 + row16 % 2)
            weight = jnp.where(pick, 1.0 / BLK, 0.0).astype(BF16)
            pooled = pooled + mm(weight, q_ref[:, g * HD : (g + 1) * HD])
        pooled = jnp.where(iota((16, HD), 0) >= 10, first, pooled)
        buf[c, z, y, 0:HALF, :] = k_ref[half * HALF : (half + 1) * HALF, :]
        buf[c, z, y, HALF:ROWS, :] = pooled.astype(BF16)

    pl.semaphore_wait(barrier, len(peers))

    own0, own1 = k0.at[c, z, y], k1.at[c, z, y]
    for n, peer in enumerate(y_peers):
        send(own0, own0, s_y0, r_y0.at[n], peer)
    for n, peer in ((0, up), (1, down)):
        send(own1, own1, s_z1, r_z1.at[1, n], peer)
    for n, peer in ((0, up), (1, down)):
        send(own0, own0, s_z0, r_z0.at[1, n, y // 2], peer)
    for peer in y_peers:
        send(own1, own1, s_y1, r_y1.at[z], peer)

    for g in range(GQ):
        scaled = (q_ref[:, g * HD : (g + 1) * HD].astype(F32) * (SCALE * LOG2E)).T
        hi, lo = split2(scaled)
        qt[g, 0:HD, :] = hi
        qt[g, HD : 2 * HD, :] = lo

    own_kk = jnp.concatenate([k_ref[...], k_ref[...]], axis=1)
    causal = iota((TOK, TOK), 0) <= iota((TOK, TOK), 1)
    for g in range(GQ):
        s = jnp.where(causal, mm(own_kk, qt[g]), NEG)
        m = jnp.max(s.reshape(4, 8, 8, TOK), axis=1)
        bmd[g] = m.reshape(32, TOK)
        top = jnp.max(m, axis=0)
        m8[g] = top
        l8[g] = jnp.sum(jnp.exp2(s.reshape(32, 8, TOK) - top[None]), axis=0)

    def z_pass(k, n):
        src_z = zz(-k) if n == 0 else zz(k)
        part = k1.at[c, src_z, y]
        wait(part, r_z1.at[k, n])
        if k < 3:
            send(part, part, s_z1, r_z1.at[k + 1, n], up if n == 0 else down)
        elif k == 3:
            @pl.when(c == n)
            def _():
                send(part, part, s_z1, r_z1.at[4, 0], up if n == 0 else down)
        for peer in y_peers:
            send(part, part, s_y1, r_y1.at[src_z], peer)

    def y_done(d):
        at = zz(d)
        wait(k1.at[c, at, 0:3], r_y1.at[at])
        send(k1.at[c, at], k1.at[c, at], s_s1, r_s1.at[at], sib)

    def bundle_pass(k, n):
        src_z = zz(-k) if n == 0 else zz(k)
        for pair in range(2):
            part = k0.at[c, src_z, 2 * pair : 2 * pair + 2]
            wait(part, r_z0.at[k, n, pair])
            if k < 3:
                send(part, part, s_z0, r_z0.at[k + 1, n, pair], up if n == 0 else down)
            elif k == 3:
                @pl.when(c == n)
                def _(part=part, pair=pair):
                    send(part, part, s_z0, r_z0.at[4, 0, pair], up if n == 0 else down)
        whole = k0.at[c, src_z]
        send(whole, whole, s_s0, r_s0.at[src_z], sib)

    for n in range(2):
        z_pass(1, n)
    for n, d in enumerate((3, 2, 1)):
        part = k0.at[c, z, yy(d)]
        wait(part, r_y0.at[n])
        for m, peer in ((0, up), (1, down)):
            send(part, part, s_z0, r_z0.at[1, m, yy(d) // 2], peer)
    send(k0.at[c, z], k0.at[c, z], s_s0, r_s0.at[z], sib)
    y_done(0)

    def z_last():
        part = k1.at[c, zz(4), y]
        wait(part, r_z1.at[4, 0])
        for peer in y_peers:
            send(part, part, s_y1, r_y1.at[zz(4)], peer)

    def bundle_last():
        for pair in range(2):
            wait(k0.at[c, zz(4), 2 * pair : 2 * pair + 2], r_z0.at[4, 0, pair])
        whole = k0.at[c, zz(4)]
        send(whole, whole, s_s0, r_s0.at[zz(4)], sib)

    events = {
        0: lambda: [z_pass(2, n) for n in range(2)],
        1: lambda: [y_done(d) for d in (-1, 1)],
        2: lambda: [bundle_pass(1, n) for n in range(2)] + [z_pass(3, n) for n in range(2)],
        3: lambda: [y_done(d) for d in (-2, 2)],
        4: lambda: z_last(),
        5: lambda: [y_done(d) for d in (-3, 3)],
        6: lambda: [bundle_pass(2, n) for n in range(2)],
        8: lambda: y_done(4),
        10: lambda: [bundle_pass(3, n) for n in range(2)],
        14: lambda: bundle_last(),
    }

    def at_slot(slot, which):
        for number, event in events.items():
            if number % 2 == which:
                @pl.when(slot == number)
                def _(event=event):
                    event()

    bufs = (k0, k1)

    def chunk(i, _):
        step = (i + 1) // 2
        zi = lax.rem(z + ZS + jnp.where(lax.rem(i, 2) == 1, -step, step), ZS)
        at_slot(2 * i, 0)
        wait(k0.at[1 - c, zi], r_s0.at[zi])
        wait(k1.at[1 - c, zi], r_s1.at[zi])
        pieces = []
        for half in range(2):
            for cc in range(2):
                piece = bufs[half][cc, zi, :, 0:HALF, :].reshape(YS * HALF, HD)
                wide = piece.astype(F32).reshape(8, BLK, HD)
                kfb[half, cc, zi, :, 0:HD] = jnp.max(wide, axis=1)
                kfb[half, cc, zi, :, HD : 2 * HD] = jnp.min(wide, axis=1)
                kfb[half, cc, zi, :, 2 * HD : 3 * HD] = jnp.sum(wide, axis=1) * (1.0 / BLK)
                pieces.append(piece)
        for cc in range(2):
            for yi in range(YS):
                mark = k0[cc, zi, yi, HALF:ROWS, :].astype(F32)[10:11, :]
                posv[cc * YS + yi] = jnp.broadcast_to(mark, (8, HD))
        keys = jnp.concatenate(pieces, axis=0)
        kk = jnp.concatenate([keys, keys], axis=1)
        for g in range(GQ):
            if g == 3:
                at_slot(2 * i + 1, 1)
            s = mm(kk, qt[g])
            top, total = m8[g], l8[g]
            for half in range(2):
                for cc in range(2):
                    base = pl.multiple_of((half * 128 + (cc * ZS + zi) * 8) * 8, 64)
                    for blk in range(8):
                        r0 = (half * 2 + cc) * 512 + blk * BLK
                        sb = s[r0 : r0 + BLK].reshape(8, 8, TOK)
                        mark = posv[cc * YS + blk // 2] < first
                        ok = jnp.concatenate([mark, mark], axis=1)
                        m = jnp.where(ok, jnp.max(sb, axis=0), NEG)
                        bm8[g, pl.ds(base + blk * 8, 8), :] = m
                        new = jnp.maximum(top, m)
                        part = jnp.sum(jnp.exp2(sb - new[None]), axis=0)
                        total = total * jnp.exp2(top - new) + jnp.where(ok, part, 0.0)
                        top = new
            m8[g] = top
            l8[g] = total
        return 0

    lax.fori_loop(0, ZS, chunk, 0)

    own = ((c * ZS + z) * YS + y) * 2
    for half in range(2):
        at = pl.multiple_of((half * 128 + own) * 8, 16)
        for g in range(GQ):
            bm8[g, pl.ds(at, 16), :] = bmd[g, half * 16 : half * 16 + 16, :]

    offs = []
    for g in range(GQ):
        m = jnp.max(m8[g], axis=0, keepdims=True)
        total = jnp.sum(l8[g] * jnp.exp2(m8[g] - m), axis=0, keepdims=True)
        offs.append(jnp.broadcast_to(m + jnp.log(total) * LOG2E, (8, TOK)))

    def merge(i, _):
        at = pl.multiple_of(i * 64, 64)
        best = None
        for g in range(GQ):
            v = bm8[g, pl.ds(at, 64), :].reshape(8, 8, TOK) - offs[g][None]
            best = v if best is None else jnp.maximum(best, v)
        best = best.reshape(64, TOK)
        for n in range(2):
            u8[n, pl.ds(at, 64), :] = best[:, n * 128 : (n + 1) * 128]
        return 0

    lax.fori_loop(0, 32, merge, 0, unroll=4)
    halves = []
    for n in range(2):
        r = u8[n, pl.ds(0, 256, stride=8), :]
        for t in range(1, 8):
            r = jnp.maximum(r, u8[n, pl.ds(t, 256, stride=8), :])
        halves.append(r.T)
    best = jnp.concatenate(halves, axis=0)
    prob = jnp.exp2(jnp.max(best.reshape(4, BLK, 256), axis=1))
    target = prob / jnp.sum(prob, axis=1, keepdims=True)
    me = z * YS + y
    tb[c, me, 0:4, :] = target[:, 0:128]
    tb[c, me, 4:8, :] = target[:, 128:256]
    mine = tb.at[c, me]
    for dz in (4, 3, 5, 2, 6, 1, 7, 0):
        for dy in (2, 1, 3, 0):
            if dz or dy:
                send(mine, mine, s_t, r_t, dev(zz(dz), yy(dy), c))

    o, kr = iota((112, 128), 0), iota((112, 128), 1)
    b = o % 4
    want_q = (b // 2) * 64 + (o % 16) // 4 * 16 + (o // 16) * 2 + b % 2
    want_i = (o % 16) // 4 * 16 + 10
    want_ii = (o % 8) // 2 * 16 + 10
    want = jnp.where(o < 80, want_q, jnp.where(o < 96, want_i, want_ii))
    pick = jnp.where(kr == want, 1.0, 0.0).astype(BF16)

    def unpack(i, _):
        cc, zi = i // ZS, lax.rem(i, ZS)
        rows = jnp.concatenate(
            [bufs[half][cc, zi, :, HALF:ROWS, :].reshape(64, HD) for half in range(2)], axis=0
        )
        got = mm(pick, rows)
        for g in range(GQ):
            pqb[g, i] = got[g * 16 : (g + 1) * 16].astype(BF16)
        posi[i] = got[80:96] + (iota((16, HD), 0) % 4).astype(F32)
        for half in range(2):
            at = 96 + half * 8
            posii[half, i] = got[at : at + 8] + (iota((8, HD), 0) % 2 + half * 2).astype(F32)
        return 0

    lax.fori_loop(0, 16, unpack, 0, unroll=4)
    pos_row = posi[...].reshape(256, HD)
    pos_col = posii[...].reshape(256, HD)
    pos_row = jnp.concatenate([pos_row, pos_row], axis=1)
    place = jnp.where(
        jnp.concatenate([pos_col, pos_col], axis=1) == iota((256, 256), 1).astype(F32), 1.0, 0.0
    ).astype(BF16)
    full = jnp.zeros((8, 256), F32)
    for term in split3(jnp.concatenate([target, target], axis=0)):
        full = full + mm(term, place)
    for n in range(4):
        map_ref[n] = full[n : n + 1]
    feats = kfb[...].reshape(256, 3 * HD).astype(BF16)
    pooled = [pqb[g].reshape(256, HD) for g in range(GQ)]
    gate_q = jnp.zeros((256, HD), F32)
    for g in range(GQ):
        gate_q = gate_q + mm(pooled[g], wq_ref[0, g * HD : (g + 1) * HD, :])
    gate_q = gate_q.astype(BF16)
    gate_k = mm(feats, wk_ref[0]).astype(BF16)
    allowed = jnp.broadcast_to(pos_col.T[0:1, :], (256, 256)) <= pos_row
    logits = jnp.where(allowed, nt(gate_q, gate_k) * SCALE, NEG)
    shifted = logits - jnp.max(logits, axis=1, keepdims=True)
    log_prob = shifted - jnp.log(jnp.sum(jnp.exp(shifted), axis=1, keepdims=True))
    gate_prob = jnp.exp(log_prob)

    wait(tb.at[c, 0:31], r_t)
    send(tb.at[c], tb.at[c], s_ts, r_ts, sib)
    wait(tb.at[1 - c], r_ts)
    tiles = tb[...].reshape(32, 2, 8, 128)
    even, odd = tiles[:, 0], tiles[:, 1]
    low = iota((32, 8, 128), 1) < 4
    left = jnp.where(low, even, pltpu.roll(odd, 4, 1))
    right = jnp.where(low, pltpu.roll(even, 4, 1), odd)
    targets = jnp.concatenate([left.reshape(256, 128), right.reshape(256, 128)], axis=1)
    loss = -jnp.sum(jnp.where(allowed, targets * log_prob, 0.0), axis=0, keepdims=True)
    loss = jnp.sum(loss, axis=1, keepdims=True)
    lx[x] = jnp.broadcast_to(loss, (8, 128))
    for n, peer in enumerate(x_peers):
        send(lx.at[x], lx.at[x], s_x.at[n], r_x.at[n], peer)
    delta = (gate_prob - targets) * SCALE
    d_hi, d_lo = split2(delta)
    q_delta = jnp.concatenate(split2(mm(d_hi, gate_k) + mm(d_lo, gate_k)), axis=1)
    k_delta = jnp.concatenate(split2(tn(d_hi, gate_q) + tn(d_lo, gate_q)), axis=1)
    for g in range(GQ):
        both = tn(pooled[g], q_delta)
        gq_ref[0, g * HD : (g + 1) * HD, :] = both[:, 0:HD] + both[:, HD:]
    both = tn(feats, k_delta)
    gk_ref[0] = both[:, 0:HD] + both[:, HD:]
    for n, d in enumerate((1, 2, 3)):
        at = lax.rem(x + XS - d, XS)
        wait(lx.at[at], r_x.at[n])
    loss_ref[...] = (lx[0] + lx[1] + lx[2] + lx[3])[0:1, 0:1] * (1.0 / (256 * XS))

    wait(k0.at[c, 0, 0:3], s_y0)
    wait(k0.at[c, 0:7], s_z0)
    wait(k0.at[c], s_s0)
    wait(k1.at[c, 0:7, 0], s_z1)
    wait(k1.at[c, 0:6], s_y1)
    wait(k1.at[c], s_s1)
    wait(tb.at[c, 0:31], s_t)
    wait(tb.at[c], s_ts)
    for n in range(3):
        wait(lx.at[x], s_x.at[n])


def per_device(queries, keys, block_position, w_gate_q, w_gate_k):
    vmem = pl.BlockSpec(memory_space=pltpu.VMEM)
    smem = pl.BlockSpec(memory_space=pltpu.SMEM)
    dma = pltpu.SemaphoreType.DMA
    target_map, grad_q, grad_k, loss = pl.pallas_call(
        kernel,
        out_shape=(
            jax.ShapeDtypeStruct((4, 1, 256), F32),
            jax.ShapeDtypeStruct((1, GQ * HD, HD), F32),
            jax.ShapeDtypeStruct((1, 3 * HD, HD), F32),
            jax.ShapeDtypeStruct((1, 1), F32),
        ),
        in_specs=[vmem, vmem, smem, vmem, vmem],
        out_specs=(vmem, vmem, vmem, vmem),
        scratch_shapes=[
            pltpu.VMEM((2, ZS, YS, ROWS, HD), BF16),
            pltpu.VMEM((2, ZS, YS, ROWS, HD), BF16),
            pltpu.VMEM((GQ, 2 * HD, TOK), BF16),
            pltpu.VMEM((GQ, 2048, TOK), F32),
            pltpu.VMEM((GQ, 32, TOK), F32),
            pltpu.VMEM((GQ, 8, TOK), F32),
            pltpu.VMEM((GQ, 8, TOK), F32),
            pltpu.VMEM((8, 8, HD), F32),
            pltpu.VMEM((2, 2, ZS, 8, 3 * HD), F32),
            pltpu.VMEM((GQ, 16, 16, HD), BF16),
            pltpu.VMEM((16, 16, HD), F32),
            pltpu.VMEM((2, 16, 8, HD), F32),
            pltpu.VMEM((2, 2048, 128), F32),
            pltpu.VMEM((2, 32, 8, 128), F32),
            pltpu.VMEM((XS, 8, 128), F32),
            dma, dma, dma, dma, dma, dma, dma, dma, dma((3,)),
            dma((3,)), dma((5, 2, 2)), dma((ZS,)), dma((5, 2)), dma((ZS,)), dma((ZS,)),
            dma, dma, dma((3,)),
        ],
        compiler_params=pltpu.CompilerParams(
            collective_id=0, has_side_effects=True, vmem_limit_bytes=50 << 20
        ),
        name="gate",
    )(queries, keys, block_position, w_gate_q, w_gate_k)
    return target_map, grad_q, grad_k, loss.reshape(())


def solution(mesh):
    return jax.shard_map(
        per_device,
        mesh=mesh,
        in_specs=(
            P("ctx", "head"),
            P("ctx", "head"),
            P("ctx"),
            P("head", None, None),
            P("head", None, None),
        ),
        out_specs=(P("ctx", "head", None), P("head", None, None), P("head", None, None), P()),
        check_vma=False,
    )
```

time: 995 us -> 65 us (0.07)
  waiting for transfers between devices: 387 us -> 0 us
  blocking collectives: 199 us -> 0 us
  loops' own time: 176 us -> 0 us
  other arithmetic: 117 us -> 0 us
  matrix products: 69.2 us -> 0 us
  Pallas kernels: 0 us -> 56.1 us
  between operations: 17.7 us -> 2.34 us
  local copies, waits for them, and re-layouts: 19.3 us -> 6.26 us
    unnamed x4 -> x0, waiting for transfers between devices: 328 us -> none
    another operation x130 -> x0, loops' own time: 176 us -> none  [the longest x2 170 us: by_shard(): return lax.fori_loop(0, shard_count, fold_one, running)]
    psum x2 -> x0, blocking collectives: 132 us -> none  [the longest x1 123 us: per_device(): lax.psum((grad_query, grad_key, loss_part), 'ctx')]
    reduce_min x128 -> x0, other arithmetic: 92.8 us -> none  [is_future(): return jnp.min(key_blocks) * BLK > jnp.max(own_pos)]
    dot_general x58 -> x0, matrix products: 69.2 us -> none  [the longest x50 64.5 us: shard_scores(): jnp.einsum('rgd,nd->grn', query_heads, one_shard, preferred_element_type=...]
    pallas_call x0 -> x1, Pallas kernels: none -> 56.1 us  [per_device(): pl.pallas_call(kernel, out_shape=(jax.ShapeDtypeStruct((4, 1, 256), F32),...]
    all_gather x1 -> x0, blocking collectives: 46 us -> none  [per_device(): all_keys = lax.all_gather(gate_key, 'ctx', axis=0, tiled=True)]
    psum x1 -> x0, waiting for transfers between devices: 45.1 us -> none  [per_device(): lax.psum((grad_query, grad_key, loss_part), 'ctx')]
  transfers between devices with their start and end apart: 3 -> 0, of which waited for: 3 -> 0; matrix products, arithmetic and copies ran while one was open for 1% -> 0% of each run, Pallas kernels for 0% -> 0%
where the time goes in v1:
time: 65 us; the launch traced here: 64.7 us
  Pallas kernels  56.1 us (86%)
  local copies, waits for them, and re-layouts  6.26 us (10%)
  between operations  2.34 us (4%)
    pallas_call x1, Pallas kernels, per_device(): pl.pallas_call(kernel, out_shape=(jax.ShapeDtypeStruct((4, 1, 256), F32),...  56.1 us
    unnamed x13, local copies, waits for them, and re-layouts  6.26 us

profile of v1, /device:TPU:1, one launch (start us, length us, event | category | flops | bytes accessed | tf_op | source)
XLA Modules:
  0.0 64.7 jit_solution(5830920525401330270)
XLA Ops:
  0.6 0.0 copy-start
  0.6 1.0 %copy-done = bf16[256,640]{1,0:T(8,128)(2,1)S(1)} copy-done((bf16[256,640]{1,0:T(8,128)(2,1)S(1)}, bf16[256,640]{1,0:T(8,128)(2,1)}, u32[]{:S(2)}) %copy-start) | copy-done | bytes 327704
  1.6 0.0 copy-start.1
  1.6 0.9 %copy-done.1 = bf16[1,640,128]{2,1,0:T(8,128)(2,1)S(1)} copy-done((bf16[1,640,128]{2,1,0:T(8,128)(2,1)S(1)}, bf16[1,640,128]{2,1,0:T(8,128)(2,1)}, u32[]{:S(2)}) %copy-start.1) | copy-done | bytes 163864
  2.5 0.0 copy-start.2
  2.5 0.9 %copy-done.2 = bf16[1,384,128]{2,1,0:T(8,128)(2,1)S(1)} copy-done((bf16[1,384,128]{2,1,0:T(8,128)(2,1)S(1)}, bf16[1,384,128]{2,1,0:T(8,128)(2,1)}, u32[]{:S(2)}) %copy-start.2) | copy-done | bytes 98328
  3.4 0.0 copy-start.3
  3.4 0.8 %copy-done.3 = bf16[256,128]{1,0:T(8,128)(2,1)S(1)} copy-done((bf16[256,128]{1,0:T(8,128)(2,1)S(1)}, bf16[256,128]{1,0:T(8,128)(2,1)}, u32[]{:S(2)}) %copy-start.3) | copy-done | bytes 65560
  4.3 0.0 copy-start.4
  4.3 0.7 %copy-done.4 = s32[4]{0:T(128)S(1)} copy-done((s32[4]{0:T(128)S(1)}, s32[4]{0:T(128)}, u32[]{:S(2)}) %copy-start.4) | copy-done | bytes 40
  4.9 56.1 %gate.1 = (f32[4,1,256]{2,1,0:T(1,128)S(1)}, f32[1,640,128]{2,1,0:T(8,128)S(1)}, f32[1,384,128]{2,1,0:T(8,128)S(1)}, f32[1,1]{1,0:T(1,128)}) custom-call(bf16[256,640]{1,0:T(8,128)(2,1)S(1)} %copy-done, bf16[256,128]{1,0:T(8,128)(2,1)S(1)} %copy-done.3, s32[4]{0:T(128)S(1)} %copy-done.4, bf16[1,640,128]{2,1,0:T(8,128)(2,1)S(1)} %copy-done.1, ...), custom_call_target="tpu_custom_call" | custom-call | tf_op jit(solution)/shard_map/gate/pallas_call | solution.py:384
  61.1 0.6 copy.13
  61.7 0.7 %copy.14 = f32[1,640,128]{2,1,0:T(8,128)} copy(f32[1,640,128]{2,1,0:T(8,128)S(1)} %get-tuple-element.17) | data formatting | bytes 655360
  62.4 0.7 %copy.15 = f32[1,384,128]{2,1,0:T(8,128)} copy(f32[1,384,128]{2,1,0:T(8,128)S(1)} %get-tuple-element.18) | data formatting | bytes 393216
Async XLA Ops:
  0.6 1.0 %copy-start = (bf16[256,640]{1,0:T(8,128)(2,1)S(1)}, bf16[256,640]{1,0:T(8,128)(2,1)}, u32[]{:S(2)}) copy-start(bf16[256,640]{1,0:T(8,128)(2,1)} %q_ref.1) | copy-start | bytes 983044
  1.6 0.9 %copy-start.1 = (bf16[1,640,128]{2,1,0:T(8,128)(2,1)S(1)}, bf16[1,640,128]{2,1,0:T(8,128)(2,1)}, u32[]{:S(2)}) copy-start(bf16[1,640,128]{2,1,0:T(8,128)(2,1)} %wq_ref.1) | copy-start | bytes 491524
  2.5 0.9 %copy-start.2 = (bf16[1,384,128]{2,1,0:T(8,128)(2,1)S(1)}, bf16[1,384,128]{2,1,0:T(8,128)(2,1)}, u32[]{:S(2)}) copy-start(bf16[1,384,128]{2,1,0:T(8,128)(2,1)} %wk_ref.1) | copy-start | bytes 294916
  3.4 0.8 %copy-start.3 = (bf16[256,128]{1,0:T(8,128)(2,1)S(1)}, bf16[256,128]{1,0:T(8,128)(2,1)}, u32[]{:S(2)}) copy-start(bf16[256,128]{1,0:T(8,128)(2,1)} %k_ref.1) | copy-start | bytes 196612
  4.3 0.7 %copy-start.4 = (s32[4]{0:T(128)S(1)}, s32[4]{0:T(128)}, u32[]{:S(2)}) copy-start(s32[4]{0:T(128)} %pos_ref.1) | copy-start | bytes 52

commit v2 on v1

v2 whole, which is shorter than its diff:
```python
import functools
import math

import jax
import jax.numpy as jnp
from jax import lax
from jax.experimental import pallas as pl
from jax.experimental.pallas import tpu as pltpu
from jax.sharding import PartitionSpec as P

ZS, YS, XS = 8, 4, 4
BLK, HD, GQ = 64, 128, 5
TOK = 256
HALF = 128
ROWS = HALF + 16
NEG = -1e30
LOG2E = 1.4426950408889634
SCALE = 1.0 / math.sqrt(HD)
F32, BF16 = jnp.float32, jnp.bfloat16
MESH = pl.DeviceIdType.MESH


def nt(a, b):
    return lax.dot_general(a, b, (((1,), (1,)), ((), ())), preferred_element_type=F32)


def tn(a, b):
    return lax.dot_general(a, b, (((0,), (0,)), ((), ())), preferred_element_type=F32)


def mm(a, b):
    return jnp.dot(a, b, preferred_element_type=F32)


def split2(a):
    hi = a.astype(BF16)
    return hi, (a - hi.astype(F32)).astype(BF16)


def split3(a):
    hi, mid = split2(a)
    return hi, mid, (a - hi.astype(F32) - mid.astype(F32)).astype(BF16)


def iota(shape, dim):
    return lax.broadcasted_iota(jnp.int32, shape, dim)


def kernel(
    q_hbm, k_hbm, pos_ref, wq_hbm, wk_hbm,
    map_hbm, gq_hbm, gk_hbm, loss_ref,
    map_ref, gq_ref, gk_ref, s_out,
    q_ref, k_ref, wq_ref, wk_ref,
    k0, k1, qt, bm8, bmd, m8, l8, posv, kfb, pqb, posi, posii, u8, tb, lx, lp, gp, gqv, s_in,
    s_y0, s_z0, s_s0, s_z1, s_y1, s_s1, s_t, s_ts, s_x,
    r_y0, r_z0, r_s0, r_z1, r_y1, r_s1, r_t, r_ts, r_x,
):
    ctx, x = lax.axis_index("ctx"), lax.axis_index("head")
    c = lax.rem(ctx, 2)
    y = lax.rem(ctx // 2, YS)
    z = ctx // (2 * YS)

    def zz(d):
        return lax.rem(z + (d + ZS), ZS)

    def yy(d):
        return lax.rem(y + d, YS)

    def dev(z_at, y_at, c_at):
        return ((z_at * YS + y_at) * 2 + c_at, x)

    up, down, sib = dev(zz(1), y, c), dev(zz(-1), y, c), dev(z, y, 1 - c)
    y_peers = [dev(z, yy(d), c) for d in (1, 2, 3)]
    other = ctx + 1 - 2 * c
    x_peers = [(at, lax.rem(x + d, XS)) for d in (1, 2, 3) for at in (ctx, other)]

    mine0, mine1 = k0.at[c, z, y], k1.at[c, z, y]
    own0, own1 = mine0.at[0:HALF], mine1.at[0:HALF]
    tile0, tile1 = mine0.at[HALF:ROWS], mine1.at[HALF:ROWS]
    keys0, keys1 = k_hbm.at[0:HALF], k_hbm.at[HALF:TOK]
    loads = [
        pltpu.make_async_copy(src, dst, s_in.at[n])
        for n, (src, dst) in enumerate(
            (
                (q_hbm, q_ref), (k_hbm, k_ref), (keys0, own0), (keys1, own1),
                (wq_hbm, wq_ref), (wk_hbm, wk_ref),
            )
        )
    ]
    for load in loads:
        load.start()
    barrier = pltpu.get_barrier_semaphore()
    peers = [up, down, sib] + y_peers + x_peers
    for peer in peers:
        pl.semaphore_signal(barrier, inc=1, device_id=peer, device_id_type=MESH)

    def send(src, dst, s_sem, r_sem, to):
        pltpu.make_async_remote_copy(
            src_ref=src, dst_ref=dst, send_sem=s_sem, recv_sem=r_sem,
            device_id=to, device_id_type=MESH,
        ).start()

    def wait(like, sem):
        pltpu.make_async_copy(like, like, sem).wait()

    def send_own(src0, dst0, src1, dst1):
        for n, peer in enumerate(y_peers):
            send(src0, dst0, s_y0, r_y0.at[n], peer)
        for n, peer in ((0, up), (1, down)):
            send(src1, dst1, s_z1, r_z1.at[1, n], peer)
        for n, peer in ((0, up), (1, down)):
            send(src0, dst0, s_z0, r_z0.at[1, n, y // 2], peer)
        for peer in y_peers:
            send(src1, dst1, s_y1, r_y1.at[z], peer)

    pl.semaphore_wait(barrier, len(peers))
    send_own(keys0, own0, keys1, own1)

    first = pos_ref[0].astype(F32)
    loads[0].wait()
    row16 = iota((16, TOK), 0)
    tok16 = iota((16, TOK), 1)
    for half, tile in ((0, tile0), (1, tile1)):
        pooled = jnp.zeros((16, HD), F32)
        for g in range(GQ):
            pick = (row16 // 2 == g) & (tok16 // BLK == half * 2 + row16 % 2)
            weight = jnp.where(pick, 1.0 / BLK, 0.0).astype(BF16)
            pooled = pooled + mm(weight, q_ref[:, g * HD : (g + 1) * HD])
        pooled = jnp.where(iota((16, HD), 0) >= 10, first, pooled)
        tile[...] = pooled.astype(BF16)
    send_own(tile0, tile0, tile1, tile1)

    for g in range(GQ):
        scaled = (q_ref[:, g * HD : (g + 1) * HD].astype(F32) * (SCALE * LOG2E)).T
        hi, lo = split2(scaled)
        qt[g, 0:HD, :] = hi
        qt[g, HD : 2 * HD, :] = lo

    for n in (1, 2, 3):
        loads[n].wait()
    own_kk = jnp.concatenate([k_ref[...], k_ref[...]], axis=1)
    causal = iota((TOK, TOK), 0) <= iota((TOK, TOK), 1)
    for g in range(GQ):
        s = jnp.where(causal, mm(own_kk, qt[g]), NEG)
        m = jnp.max(s.reshape(4, 8, 8, TOK), axis=1)
        bmd[g] = m.reshape(32, TOK)
        top = jnp.max(m, axis=0)
        m8[g] = top
        l8[g] = jnp.sum(jnp.exp2(s.reshape(32, 8, TOK) - top[None]), axis=0)

    def z_pass(k):
        for n, src_z in ((0, zz(-k)), (1, zz(k))):
            part = k1.at[c, src_z, y]
            wait(part, r_z1.at[k, n])
            if k < 3:
                send(part, part, s_z1, r_z1.at[k + 1, n], up if n == 0 else down)
            else:
                @pl.when(c == n)
                def _(part=part, n=n):
                    send(part, part, s_z1, r_z1.at[4, 0], up if n == 0 else down)
            for peer in y_peers:
                send(part, part, s_y1, r_y1.at[src_z], peer)

    def y_done(d):
        at = zz(d)
        wait(k1.at[c, at, 0:3], r_y1.at[at])
        send(k1.at[c, at], k1.at[c, at], s_s1, r_s1.at[at], sib)

    def bundle_pass(k, p):
        pair = lax.rem(y // 2 + p, 2)
        for n, src_z in ((0, zz(-k)), (1, zz(k))):
            part = k0.at[c, src_z, pl.ds(2 * pair, 2)]
            wait(part, r_z0.at[k, n, pair])
            if k < 3:
                send(part, part, s_z0, r_z0.at[k + 1, n, pair], up if n == 0 else down)
            else:
                @pl.when(c == n)
                def _(part=part, n=n):
                    send(part, part, s_z0, r_z0.at[4, 0, pair], up if n == 0 else down)
        if p == 1:
            for src_z in (zz(-k), zz(k)):
                send(k0.at[c, src_z], k0.at[c, src_z], s_s0, r_s0.at[src_z], sib)

    def bundle_last():
        for pair in range(2):
            wait(k0.at[c, zz(4), 2 * pair : 2 * pair + 2], r_z0.at[4, 0, pair])
        whole = k0.at[c, zz(4)]
        send(whole, whole, s_s0, r_s0.at[zz(4)], sib)

    def z_last():
        part = k1.at[c, zz(4), y]
        wait(part, r_z1.at[4, 0])
        for peer in y_peers:
            send(part, part, s_y1, r_y1.at[zz(4)], peer)

    def y_pass(d):
        part = k0.at[c, z, yy(d)]
        wait(part, r_y0.at[3 - d])
        for n, peer in ((0, up), (1, down)):
            send(part, part, s_z0, r_z0.at[1, n, yy(d) // 2], peer)

    y_pass(3)
    y_pass(1)
    z_pass(1)
    y_pass(2)
    send(k0.at[c, z], k0.at[c, z], s_s0, r_s0.at[z], sib)
    y_done(0)

    bufs = (k0, k1)

    def attend(cc, zs):
        pieces = []
        for half in range(2):
            for zi in zs:
                piece = bufs[half][cc, zi, :, 0:HALF, :].reshape(YS * HALF, HD)
                wide = piece.astype(F32).reshape(8, BLK, HD)
                kfb[half, cc, zi, :, 0:HD] = jnp.max(wide, axis=1)
                kfb[half, cc, zi, :, HD : 2 * HD] = jnp.min(wide, axis=1)
                kfb[half, cc, zi, :, 2 * HD : 3 * HD] = jnp.sum(wide, axis=1) * (1.0 / BLK)
                pieces.append(piece)
        for n, zi in enumerate(zs):
            for yi in range(YS):
                mark = k0[cc, zi, yi, HALF:ROWS, :].astype(F32)[10:11, :]
                posv[n * YS + yi] = jnp.broadcast_to(mark, (8, HD))
        keys = jnp.concatenate(pieces, axis=0)
        kk = jnp.concatenate([keys, keys], axis=1)
        for g in range(GQ):
            s = mm(kk, qt[g])
            for side in range(2):
                cols = slice(side * 128, side * 128 + 128)
                top, total = m8[g, :, cols], l8[g, :, cols]
                for half in range(2):
                    for n, zi in enumerate(zs):
                        base = pl.multiple_of((half * 128 + (cc * ZS + zi) * 8) * 8, 64)
                        for yi in range(YS):
                            r0 = ((half * len(zs) + n) * YS + yi) * HALF
                            sb = s[r0 : r0 + HALF, cols].reshape(16, 8, 128)
                            ok = posv[n * YS + yi] < first
                            new = top
                            for blk in range(2):
                                m = jnp.max(sb[blk * 8 : blk * 8 + 8], axis=0)
                                m = jnp.where(ok, m, NEG)
                                bm8[g, pl.ds(base + (yi * 2 + blk) * 8, 8), cols] = m
                                new = jnp.maximum(new, m)
                            part = jnp.sum(jnp.exp2(sb - new[None]), axis=0)
                            total = total * jnp.exp2(top - new) + jnp.where(ok, part, 0.0)
                            top = new
                m8[g, :, cols] = top
                l8[g, :, cols] = total

    def both_cores(d):
        def one(j, _):
            cc = lax.rem(c + j, 2)

            @pl.when(j == 1)
            def _():
                if d == 0:
                    bundle_pass(1, 0)
                    z_pass(2)
                wait(k0.at[1 - c, zz(d)], r_s0.at[zz(d)])
                wait(k1.at[1 - c, zz(d)], r_s1.at[zz(d)])

            attend(cc, [zz(d)])
            return 0

        lax.fori_loop(0, 2, one, 0)

    def at_step(i, events):
        for number, event in events.items():
            @pl.when(i == number)
            def _(event=event):
                event()

    def pair_step(i, _):
        k, j = i // 2 + 1, lax.rem(i, 2)
        cc = lax.rem(c + j, 2)
        zs = [lax.rem(z + ZS - k, ZS), lax.rem(z + k, ZS)]
        at_step(i, {
            0: lambda: [bundle_pass(1, 1)] + [y_done(d) for d in (-1, 1)],
            1: lambda: [bundle_pass(2, 0), z_pass(3)],
            2: lambda: [bundle_pass(2, 1)] + [y_done(d) for d in (-2, 2)],
            3: lambda: [bundle_pass(3, 0), z_last()],
            4: lambda: [y_done(d) for d in (-3, 3)] + [bundle_pass(3, 1)],
            5: lambda: y_done(4),
        })

        @pl.when(j == 1)
        def _():
            for zi in zs:
                wait(k0.at[1 - c, zi], r_s0.at[zi])
                wait(k1.at[1 - c, zi], r_s1.at[zi])

        attend(cc, zs)
        return 0

    both_cores(0)
    lax.fori_loop(0, 6, pair_step, 0)
    bundle_last()
    both_cores(4)

    own = ((c * ZS + z) * YS + y) * 2
    for half in range(2):
        at = pl.multiple_of((half * 128 + own) * 8, 16)
        for g in range(GQ):
            bm8[g, pl.ds(at, 16), :] = bmd[g, half * 16 : half * 16 + 16, :]

    offs = []
    for g in range(GQ):
        m = jnp.max(m8[g], axis=0, keepdims=True)
        total = jnp.sum(l8[g] * jnp.exp2(m8[g] - m), axis=0, keepdims=True)
        offs.append(jnp.broadcast_to(m + jnp.log(total) * LOG2E, (8, TOK)))

    def merge(i, _):
        at = pl.multiple_of(i * 64, 64)
        best = None
        for g in range(GQ):
            v = bm8[g, pl.ds(at, 64), :].reshape(8, 8, TOK) - offs[g][None]
            best = v if best is None else jnp.maximum(best, v)
        best = best.reshape(64, TOK)
        for n in range(2):
            u8[n, pl.ds(at, 64), :] = best[:, n * 128 : (n + 1) * 128]
        return 0

    lax.fori_loop(0, 32, merge, 0, unroll=4)
    halves = []
    for n in range(2):
        r = u8[n, pl.ds(0, 256, stride=8), :]
        for t in range(1, 8):
            r = jnp.maximum(r, u8[n, pl.ds(t, 256, stride=8), :])
        halves.append(r.T)
    best = jnp.concatenate(halves, axis=0)
    prob = jnp.exp2(jnp.max(best.reshape(4, BLK, 256), axis=1))
    target = prob / jnp.sum(prob, axis=1, keepdims=True)
    me = z * YS + y
    tb[c, me, 0:4, :] = target[:, 0:128]
    tb[c, me, 4:8, :] = target[:, 128:256]
    mine = tb.at[c, me]
    for dz in (4, 3, 5, 2, 6, 1, 7, 0):
        for dy in (2, 1, 3, 0):
            if dz or dy:
                send(mine, mine, s_t, r_t.at[z], dev(zz(dz), yy(dy), c))

    o, kr = iota((112, 128), 0), iota((112, 128), 1)
    b = o % 4
    want_q = (b // 2) * 64 + (o % 16) // 4 * 16 + (o // 16) * 2 + b % 2
    want_i = (o % 16) // 4 * 16 + 10
    want_ii = (o % 8) // 2 * 16 + 10
    want = jnp.where(o < 80, want_q, jnp.where(o < 96, want_i, want_ii))
    pick = jnp.where(kr == want, 1.0, 0.0).astype(BF16)

    def unpack(i, _):
        cc, zi = i // ZS, lax.rem(i, ZS)
        rows = jnp.concatenate(
            [bufs[half][cc, zi, :, HALF:ROWS, :].reshape(64, HD) for half in range(2)], axis=0
        )
        got = mm(pick, rows)
        for g in range(GQ):
            pqb[g, i] = got[g * 16 : (g + 1) * 16].astype(BF16)
        posi[i] = got[80:96] + (iota((16, HD), 0) % 4).astype(F32)
        for half in range(2):
            at = 96 + half * 8
            posii[half, i] = got[at : at + 8] + (iota((8, HD), 0) % 2 + half * 2).astype(F32)
        return 0

    lax.fori_loop(0, 16, unpack, 0, unroll=4)
    pos_row = posi[...].reshape(256, HD)
    pos_col = posii[...].reshape(256, HD)
    pos_row = jnp.concatenate([pos_row, pos_row], axis=1)
    place = jnp.where(
        jnp.concatenate([pos_col, pos_col], axis=1) == iota((256, 256), 1).astype(F32), 1.0, 0.0
    ).astype(BF16)
    full = jnp.zeros((8, 256), F32)
    for term in split3(jnp.concatenate([target, target], axis=0)):
        full = full + mm(term, place)
    for n in range(4):
        map_ref[n] = full[n : n + 1]
    stores = [
        pltpu.make_async_copy(src, dst, s_out.at[n])
        for n, (src, dst) in enumerate(((map_ref, map_hbm), (gq_ref, gq_hbm), (gk_ref, gk_hbm)))
    ]
    stores[0].start()
    loads[4].wait()
    loads[5].wait()
    feats = kfb[...].reshape(256, 3 * HD).astype(BF16)
    gate_q = jnp.zeros((256, HD), F32)
    for g in range(GQ):
        gate_q = gate_q + mm(pqb[g].reshape(256, HD), wq_ref[0, g * HD : (g + 1) * HD, :])
    gate_q = gate_q.astype(BF16)
    gate_k = mm(feats, wk_ref[0]).astype(BF16)
    allowed = jnp.broadcast_to(pos_col.T[0:1, :], (256, 256)) <= pos_row
    logits = jnp.where(allowed, nt(gate_q, gate_k) * SCALE, NEG)
    shifted = logits - jnp.max(logits, axis=1, keepdims=True)
    log_prob = shifted - jnp.log(jnp.sum(jnp.exp(shifted), axis=1, keepdims=True))
    gqv[...] = gate_q
    gp[...] = jnp.exp(log_prob)
    lp[...] = jnp.where(allowed, log_prob, 0.0)

    def rows_of(cc):
        at = pl.ds(pl.multiple_of(cc * 128, 128), 128)
        tiles = tb[cc].reshape(16, 2, 8, 128)
        even, odd = tiles[:, 0], tiles[:, 1]
        low = iota((16, 8, 128), 1) < 4
        left = jnp.where(low, even, pltpu.roll(odd, 4, 1))
        right = jnp.where(low, pltpu.roll(even, 4, 1), odd)
        return at, jnp.concatenate([left.reshape(128, 128), right.reshape(128, 128)], axis=1)

    def terms(cc, at, targets):
        delta = (gp[at, :] - targets) * SCALE
        d_hi, d_lo = split2(delta)
        q_delta = jnp.concatenate(split2(mm(d_hi, gate_k) + mm(d_lo, gate_k)), axis=1)
        grads = []
        for g in range(GQ):
            pooled = pqb[g, pl.ds(pl.multiple_of(cc * ZS, ZS), ZS)].reshape(128, HD)
            both = tn(pooled, q_delta)
            grads.append(both[:, 0:HD] + both[:, HD:])
        return grads, tn(d_hi, gqv[at, :]) + tn(d_lo, gqv[at, :])

    for d in (0, 1, -1, 2, -2, 3, -3, 4):
        part = tb.at[c, pl.ds(zz(d) * YS, YS)]
        wait(tb.at[c, pl.ds(zz(d) * YS, YS if d else YS - 1)], r_t.at[zz(d)])
        send(part, part, s_ts, r_ts, sib)
    at, targets = rows_of(c)
    loss = -jnp.sum(targets * lp[at, :], axis=0, keepdims=True)
    loss = jnp.sum(loss, axis=1, keepdims=True)
    slot = c * XS + x
    lx[slot] = jnp.broadcast_to(loss, (8, 128))
    for peer in x_peers + [sib]:
        send(lx.at[slot], lx.at[slot], s_x, r_x, peer)
    near, k_near = terms(c, at, targets)
    for g in range(GQ):
        gq_ref[0, g * HD : (g + 1) * HD, :] = near[g]
    wait(tb.at[1 - c], r_ts)
    at, targets = rows_of(1 - c)
    far, k_far = terms(1 - c, at, targets)
    for g in range(GQ):
        gq_ref[0, g * HD : (g + 1) * HD, :] += far[g]
    stores[1].start()
    both = tn(feats, jnp.concatenate(split2(k_near + k_far), axis=1))
    gk_ref[0] = both[:, 0:HD] + both[:, HD:]
    stores[2].start()
    wait(lx.at[0:7], r_x)
    total = lx[0]
    for n in range(1, 2 * XS):
        total = total + lx[n]
    loss_ref[...] = total[0:1, 0:1] * (1.0 / (256 * XS))

    for store in stores:
        store.wait()
    wait(k0.at[c, 0, 0:3], s_y0)
    wait(k0.at[c, 0:7], s_z0)
    wait(k0.at[c], s_s0)
    wait(k1.at[c, 0:7, 0], s_z1)
    wait(k1.at[c, 0:6], s_y1)
    wait(k1.at[c], s_s1)
    wait(tb.at[c, 0:31], s_t)
    wait(tb.at[c], s_ts)
    wait(lx.at[0:7], s_x)


def place_results(
    map_in, gq_in, gk_in, loss_in, map_out, gq_out, gk_out, loss_out, map_v, gq_v, gk_v, sems
):
    through = ((gq_in, gq_v, gq_out), (gk_in, gk_v, gk_out), (map_in, map_v, map_out))
    into = [pltpu.make_async_copy(src, mid, sems.at[0, n]) for n, (src, mid, _) in enumerate(through)]
    out = [pltpu.make_async_copy(mid, dst, sems.at[1, n]) for n, (_, mid, dst) in enumerate(through)]
    for copy in into:
        copy.start()
    loss_out[...] = loss_in[...]
    for first, second in zip(into, out):
        first.wait()
        second.start()
    for copy in out:
        copy.wait()


def per_device(queries, keys, block_position, w_gate_q, w_gate_k):
    vmem = pl.BlockSpec(memory_space=pltpu.VMEM)
    smem = pl.BlockSpec(memory_space=pltpu.SMEM)
    hbm = pl.BlockSpec(memory_space=pltpu.HBM)
    dma = pltpu.SemaphoreType.DMA
    target_map, grad_q, grad_k, loss = pl.pallas_call(
        kernel,
        out_shape=(
            jax.ShapeDtypeStruct((4, 1, 256), F32),
            jax.ShapeDtypeStruct((1, GQ * HD, HD), F32),
            jax.ShapeDtypeStruct((1, 3 * HD, HD), F32),
            jax.ShapeDtypeStruct((1, 1), F32),
        ),
        in_specs=[hbm, hbm, smem, hbm, hbm],
        out_specs=(hbm, hbm, hbm, vmem),
        scratch_shapes=[
            pltpu.VMEM((4, 1, 256), F32),
            pltpu.VMEM((1, GQ * HD, HD), F32),
            pltpu.VMEM((1, 3 * HD, HD), F32),
            dma((3,)),
            pltpu.VMEM((TOK, GQ * HD), BF16),
            pltpu.VMEM((TOK, HD), BF16),
            pltpu.VMEM((1, GQ * HD, HD), BF16),
            pltpu.VMEM((1, 3 * HD, HD), BF16),
            pltpu.VMEM((2, ZS, YS, ROWS, HD), BF16),
            pltpu.VMEM((2, ZS, YS, ROWS, HD), BF16),
            pltpu.VMEM((GQ, 2 * HD, TOK), BF16),
            pltpu.VMEM((GQ, 2048, TOK), F32),
            pltpu.VMEM((GQ, 32, TOK), F32),
            pltpu.VMEM((GQ, 8, TOK), F32),
            pltpu.VMEM((GQ, 8, TOK), F32),
            pltpu.VMEM((8, 8, HD), F32),
            pltpu.VMEM((2, 2, ZS, 8, 3 * HD), F32),
            pltpu.VMEM((GQ, 16, 16, HD), BF16),
            pltpu.VMEM((16, 16, HD), F32),
            pltpu.VMEM((2, 16, 8, HD), F32),
            pltpu.VMEM((2, 2048, 128), F32),
            pltpu.VMEM((2, 32, 8, 128), F32),
            pltpu.VMEM((2 * XS, 8, 128), F32),
            pltpu.VMEM((256, 256), F32),
            pltpu.VMEM((256, 256), F32),
            pltpu.VMEM((256, HD), BF16),
            dma((6,)),
            dma, dma, dma, dma, dma, dma, dma, dma, dma,
            dma((3,)), dma((5, 2, 2)), dma((ZS,)), dma((5, 2)), dma((ZS,)), dma((ZS,)),
            dma((ZS,)), dma, dma,
        ],
        compiler_params=pltpu.CompilerParams(
            collective_id=0, has_side_effects=True, vmem_limit_bytes=63 << 20
        ),
        name="gate",
    )(queries, keys, block_position, w_gate_q, w_gate_k)
    hbm_out = (
        jax.ShapeDtypeStruct((4, 1, 256), F32),
        jax.ShapeDtypeStruct((1, GQ * HD, HD), F32),
        jax.ShapeDtypeStruct((1, 3 * HD, HD), F32),
        jax.ShapeDtypeStruct((1, 1), F32),
    )
    target_map, grad_q, grad_k, loss = pl.pallas_call(
        place_results,
        out_shape=hbm_out,
        in_specs=[hbm, hbm, hbm, vmem],
        out_specs=(hbm, hbm, hbm, vmem),
        scratch_shapes=[
            pltpu.VMEM((4, 1, 256), F32),
            pltpu.VMEM((1, GQ * HD, HD), F32),
            pltpu.VMEM((1, 3 * HD, HD), F32),
            dma((2, 3)),
        ],
        compiler_params=pltpu.CompilerParams(vmem_limit_bytes=63 << 20),
        name="place",
    )(target_map, grad_q, grad_k, loss)
    return target_map, grad_q, grad_k, loss.reshape(())


def solution(mesh):
    return jax.shard_map(
        per_device,
        mesh=mesh,
        in_specs=(
            P("ctx", "head"),
            P("ctx", "head"),
            P("ctx"),
            P("head", None, None),
            P("head", None, None),
        ),
        out_specs=(P("ctx", "head", None), P("head", None, None), P("head", None, None), P()),
        check_vma=False,
    )
```

time: 65 us -> 54.4 us (0.84)
  local copies, waits for them, and re-layouts: 6.26 us -> 0 us
  Pallas kernels: 56.1 us -> 53.7 us
  between operations: 2.34 us -> 0.64 us
    unnamed x13 -> x0, local copies, waits for them, and re-layouts: 6.26 us -> none
    pallas_call x1, Pallas kernels: 56.1 us -> 50.8 us  [per_device(): pl.pallas_call(kernel, out_shape=(jax.ShapeDtypeStruct((4, 1, 256), F32),...]
    pallas_call x0 -> x1, Pallas kernels: none -> 2.93 us  [per_device(): pl.pallas_call(place_results, out_shape=hbm_out, in_specs=[hbm, hbm, hbm,...]
where the time goes in v2:
time: 54.4 us; the launch traced here: 54.3 us
  Pallas kernels  53.7 us (99%)
  between operations  0.64 us (1%)
    pallas_call x1, Pallas kernels, per_device(): pl.pallas_call(kernel, out_shape=(jax.ShapeDtypeStruct((4, 1, 256), F32),...  50.8 us
    pallas_call x1, Pallas kernels, per_device(): pl.pallas_call(place_results, out_shape=hbm_out, in_specs=[hbm, hbm, hbm,...  2.93 us

profile of v2, /device:TPU:1, one launch (start us, length us, event | category | flops | bytes accessed | tf_op | source)
XLA Modules:
  0.0 54.3 jit_solution(6155353605201673999)
XLA Ops:
  0.6 50.8 %gate.1 = (f32[4,1,256]{2,1,0:T(1,128)}, f32[1,640,128]{2,1,0:T(8,128)}, f32[1,384,128]{2,1,0:T(8,128)}, f32[1,1]{1,0:T(1,128)}) custom-call(bf16[256,640]{1,0:T(8,128)(2,1)} %q_hbm.1, bf16[256,128]{1,0:T(8,128)(2,1)} %k_hbm.1, s32[4]{0:T(128)} %pos_ref.1, bf16[1,640,128]{2,1,0:T(8,128)(2,1)} %wq_hbm.1, bf16[1,384,128]{2,1,0:T(8,128)(2,1)} %wk_hbm.1), custom_call_target="tpu_custom_call" | custom-call | tf_op jit(solution)/shard_map/gate/pallas_call | solution.py:481
  51.4 2.9 %place.1 = (f32[4,1,256]{2,1,0:T(1,128)}, f32[1,640,128]{2,1,0:T(8,128)}, f32[1,384,128]{2,1,0:T(8,128)}, f32[1,1]{1,0:T(1,128)}) custom-call(f32[4,1,256]{2,1,0:T(1,128)} %get-tuple-element.12.map_in, f32[1,640,128]{2,1,0:T(8,128)} %get-tuple-element.13.gq_in, f32[1,384,128]{2,1,0:T(8,128)} %get-tuple-element.14.gk_in, f32[1,1]{1,0:T(1,128)} %get-tuple-element.15.loss_in), custom_call_target="tpu_custom_call" | custom-call | tf_op jit(solution)/shard_map/place/pallas_call | solution.py:534

commit v3 on v2

--- a/solution.py
+++ b/solution.py
@@ -47,9 +47,9 @@
 
 
 def kernel(
-    q_hbm, k_hbm, pos_ref, wq_hbm, wk_hbm,
-    map_hbm, gq_hbm, gk_hbm, loss_ref,
-    map_ref, gq_ref, gk_ref, s_out,
+    q_hbm, k_hbm, pos_hbm, wq_hbm, wk_hbm,
+    map_hbm, gq_hbm, gk_hbm, loss_hbm,
+    map_ref, gq_ref, gk_ref, loss_ref, pos_ref, s_out,
     q_ref, k_ref, wq_ref, wk_ref,
     k0, k1, qt, bm8, bmd, m8, l8, posv, kfb, pqb, posi, posii, u8, tb, lx, lp, gp, gqv, s_in,
     s_y0, s_z0, s_s0, s_z1, s_y1, s_s1, s_t, s_ts, s_x,
@@ -74,6 +74,11 @@
     other = ctx + 1 - 2 * c
     x_peers = [(at, lax.rem(x + d, XS)) for d in (1, 2, 3) for at in (ctx, other)]
 
+    barrier = pltpu.get_barrier_semaphore()
+    peers = [up, down, sib] + y_peers + x_peers
+    for peer in peers:
+        pl.semaphore_signal(barrier, inc=1, device_id=peer, device_id_type=MESH)
+
     mine0, mine1 = k0.at[c, z, y], k1.at[c, z, y]
     own0, own1 = mine0.at[0:HALF], mine1.at[0:HALF]
     tile0, tile1 = mine0.at[HALF:ROWS], mine1.at[HALF:ROWS]
@@ -83,17 +88,12 @@
         for n, (src, dst) in enumerate(
             (
                 (q_hbm, q_ref), (k_hbm, k_ref), (keys0, own0), (keys1, own1),
-                (wq_hbm, wq_ref), (wk_hbm, wk_ref),
+                (wq_hbm, wq_ref), (wk_hbm, wk_ref), (pos_hbm, pos_ref),
             )
         )
     ]
     for load in loads:
         load.start()
-    barrier = pltpu.get_barrier_semaphore()
-    peers = [up, down, sib] + y_peers + x_peers
-    for peer in peers:
-        pl.semaphore_signal(barrier, inc=1, device_id=peer, device_id_type=MESH)
-
     def send(src, dst, s_sem, r_sem, to):
         pltpu.make_async_remote_copy(
             src_ref=src, dst_ref=dst, send_sem=s_sem, recv_sem=r_sem,
@@ -116,6 +116,7 @@
     pl.semaphore_wait(barrier, len(peers))
     send_own(keys0, own0, keys1, own1)
 
+    loads[6].wait()
     first = pos_ref[0].astype(F32)
     loads[0].wait()
     row16 = iota((16, TOK), 0)
@@ -376,7 +377,9 @@
         map_ref[n] = full[n : n + 1]
     stores = [
         pltpu.make_async_copy(src, dst, s_out.at[n])
-        for n, (src, dst) in enumerate(((map_ref, map_hbm), (gq_ref, gq_hbm), (gk_ref, gk_hbm)))
+        for n, (src, dst) in enumerate(
+            ((map_ref, map_hbm), (gq_ref, gq_hbm), (gk_ref, gk_hbm), (loss_ref, loss_hbm))
+        )
     ]
     stores[0].start()
     loads[4].wait()
@@ -443,9 +446,8 @@
     for n in range(1, 2 * XS):
         total = total + lx[n]
     loss_ref[...] = total[0:1, 0:1] * (1.0 / (256 * XS))
-
-    for store in stores:
-        store.wait()
+    stores[3].start()
+
     wait(k0.at[c, 0, 0:3], s_y0)
     wait(k0.at[c, 0:7], s_z0)
     wait(k0.at[c], s_s0)
@@ -455,17 +457,22 @@
     wait(tb.at[c, 0:31], s_t)
     wait(tb.at[c], s_ts)
     wait(lx.at[0:7], s_x)
+    for store in stores:
+        store.wait()
 
 
 def place_results(
-    map_in, gq_in, gk_in, loss_in, map_out, gq_out, gk_out, loss_out, map_v, gq_v, gk_v, sems
+    map_in, gq_in, gk_in, loss_in, map_out, gq_out, gk_out, loss_out,
+    map_v, gq_v, gk_v, loss_v, sems,
 ):
-    through = ((gq_in, gq_v, gq_out), (gk_in, gk_v, gk_out), (map_in, map_v, map_out))
+    through = (
+        (gq_in, gq_v, gq_out), (gk_in, gk_v, gk_out),
+        (map_in, map_v, map_out), (loss_in, loss_v, loss_out),
+    )
     into = [pltpu.make_async_copy(src, mid, sems.at[0, n]) for n, (src, mid, _) in enumerate(through)]
     out = [pltpu.make_async_copy(mid, dst, sems.at[1, n]) for n, (_, mid, dst) in enumerate(through)]
     for copy in into:
         copy.start()
-    loss_out[...] = loss_in[...]
     for first, second in zip(into, out):
         first.wait()
         second.start()
@@ -474,8 +481,6 @@
 
 
 def per_device(queries, keys, block_position, w_gate_q, w_gate_k):
-    vmem = pl.BlockSpec(memory_space=pltpu.VMEM)
-    smem = pl.BlockSpec(memory_space=pltpu.SMEM)
     hbm = pl.BlockSpec(memory_space=pltpu.HBM)
     dma = pltpu.SemaphoreType.DMA
     target_map, grad_q, grad_k, loss = pl.pallas_call(
@@ -486,13 +491,15 @@
             jax.ShapeDtypeStruct((1, 3 * HD, HD), F32),
             jax.ShapeDtypeStruct((1, 1), F32),
         ),
-        in_specs=[hbm, hbm, smem, hbm, hbm],
-        out_specs=(hbm, hbm, hbm, vmem),
+        in_specs=[hbm, hbm, hbm, hbm, hbm],
+        out_specs=(hbm, hbm, hbm, hbm),
         scratch_shapes=[
             pltpu.VMEM((4, 1, 256), F32),
             pltpu.VMEM((1, GQ * HD, HD), F32),
             pltpu.VMEM((1, 3 * HD, HD), F32),
-            dma((3,)),
+            pltpu.VMEM((1, 1), F32),
+            pltpu.SMEM((4,), jnp.int32),
+            dma((4,)),
             pltpu.VMEM((TOK, GQ * HD), BF16),
             pltpu.VMEM((TOK, HD), BF16),
             pltpu.VMEM((1, GQ * HD, HD), BF16),
@@ -515,7 +522,7 @@
             pltpu.VMEM((256, 256), F32),
             pltpu.VMEM((256, 256), F32),
             pltpu.VMEM((256, HD), BF16),
-            dma((6,)),
+            dma((7,)),
             dma, dma, dma, dma, dma, dma, dma, dma, dma,
             dma((3,)), dma((5, 2, 2)), dma((ZS,)), dma((5, 2)), dma((ZS,)), dma((ZS,)),
             dma((ZS,)), dma, dma,
@@ -534,13 +541,14 @@
     target_map, grad_q, grad_k, loss = pl.pallas_call(
         place_results,
         out_shape=hbm_out,
-        in_specs=[hbm, hbm, hbm, vmem],
-        out_specs=(hbm, hbm, hbm, vmem),
+        in_specs=[hbm, hbm, hbm, hbm],
+        out_specs=(hbm, hbm, hbm, hbm),
         scratch_shapes=[
             pltpu.VMEM((4, 1, 256), F32),
             pltpu.VMEM((1, GQ * HD, HD), F32),
             pltpu.VMEM((1, 3 * HD, HD), F32),
-            dma((2, 3)),
+            pltpu.VMEM((1, 1), F32),
+            dma((2, 4)),
         ],
         compiler_params=pltpu.CompilerParams(vmem_limit_bytes=63 << 20),
         name="place",

time: 54.4 us -> 53.3 us (0.980)
  Pallas kernels: 53.7 us -> 52.5 us
    pallas_call x1, Pallas kernels: 50.8 us -> 50.1 us  [per_device(): pl.pallas_call(kernel, out_shape=(jax.ShapeDtypeStruct((4, 1, 256), F32),...]
where the time goes in v3:
time: 53.3 us; the launch traced here: 53.2 us
  Pallas kernels  52.5 us (98%)
  between operations  0.64 us (1%)
    pallas_call x1, Pallas kernels, per_device(): pl.pallas_call(kernel, out_shape=(jax.ShapeDtypeStruct((4, 1, 256), F32),...  50.1 us
    pallas_call x1, Pallas kernels, per_device(): pl.pallas_call(place_results, out_shape=hbm_out, in_specs=[hbm, hbm, hbm,...  2.44 us

profile of v3, /device:TPU:1, one launch (start us, length us, event | category | flops | bytes accessed | tf_op | source)
XLA Modules:
  0.0 53.2 jit_solution(18222138511895376394)
XLA Ops:
  0.6 50.1 %gate.1 = (f32[4,1,256]{2,1,0:T(1,128)}, f32[1,640,128]{2,1,0:T(8,128)}, f32[1,384,128]{2,1,0:T(8,128)}, f32[1,1]{1,0:T(1,128)}) custom-call(bf16[256,640]{1,0:T(8,128)(2,1)} %q_hbm.1, bf16[256,128]{1,0:T(8,128)(2,1)} %k_hbm.1, s32[4]{0:T(128)} %pos_hbm.1, bf16[1,640,128]{2,1,0:T(8,128)(2,1)} %wq_hbm.1, bf16[1,384,128]{2,1,0:T(8,128)(2,1)} %wk_hbm.1), custom_call_target="tpu_custom_call" | custom-call | tf_op jit(solution)/shard_map/gate/pallas_call | solution.py:486
  50.7 2.4 %place.1 = (f32[4,1,256]{2,1,0:T(1,128)}, f32[1,640,128]{2,1,0:T(8,128)}, f32[1,384,128]{2,1,0:T(8,128)}, f32[1,1]{1,0:T(1,128)}) custom-call(f32[4,1,256]{2,1,0:T(1,128)} %get-tuple-element.12.map_in, f32[1,640,128]{2,1,0:T(8,128)} %get-tuple-element.13.gq_in, f32[1,384,128]{2,1,0:T(8,128)} %get-tuple-element.14.gk_in, f32[1,1]{1,0:T(1,128)} %get-tuple-element.15.loss_in), custom_call_target="tpu_custom_call" | custom-call | tf_op jit(solution)/shard_map/place/pallas_call | solution.py:541

commit v4 on v3

--- a/solution.py
+++ b/solution.py
@@ -322,7 +322,7 @@
             u8[n, pl.ds(at, 64), :] = best[:, n * 128 : (n + 1) * 128]
         return 0
 
-    lax.fori_loop(0, 32, merge, 0, unroll=4)
+    lax.fori_loop(0, 32, merge, 0, unroll=8)
     halves = []
     for n in range(2):
         r = u8[n, pl.ds(0, 256, stride=8), :]
@@ -465,9 +465,11 @@
     map_in, gq_in, gk_in, loss_in, map_out, gq_out, gk_out, loss_out,
     map_v, gq_v, gk_v, loss_v, sems,
 ):
+    half = pl.ds(0, GQ * HD // 2), pl.ds(GQ * HD // 2, GQ * HD // 2)
     through = (
-        (gq_in, gq_v, gq_out), (gk_in, gk_v, gk_out),
-        (map_in, map_v, map_out), (loss_in, loss_v, loss_out),
+        (loss_in, loss_v, loss_out), (map_in, map_v, map_out), (gk_in, gk_v, gk_out),
+        (gq_in.at[:, half[0]], gq_v.at[:, half[0]], gq_out.at[:, half[0]]),
+        (gq_in.at[:, half[1]], gq_v.at[:, half[1]], gq_out.at[:, half[1]]),
     )
     into = [pltpu.make_async_copy(src, mid, sems.at[0, n]) for n, (src, mid, _) in enumerate(through)]
     out = [pltpu.make_async_copy(mid, dst, sems.at[1, n]) for n, (_, mid, dst) in enumerate(through)]
@@ -548,7 +550,7 @@
             pltpu.VMEM((1, GQ * HD, HD), F32),
             pltpu.VMEM((1, 3 * HD, HD), F32),
             pltpu.VMEM((1, 1), F32),
-            dma((2, 4)),
+            dma((2, 5)),
         ],
         compiler_params=pltpu.CompilerParams(vmem_limit_bytes=63 << 20),
         name="place",

time: 53.3 us -> 53.3 us (level)
  no operation moved by 1% of the time
where the time goes in v4:
time: 53.3 us; the launch traced here: 53.2 us
  Pallas kernels  52.5 us (98%)
  between operations  0.64 us (1%)
    pallas_call x1, Pallas kernels, per_device(): pl.pallas_call(kernel, out_shape=(jax.ShapeDtypeStruct((4, 1, 256), F32),...  50.1 us
    pallas_call x1, Pallas kernels, per_device(): pl.pallas_call(place_results, out_shape=hbm_out, in_specs=[hbm, hbm, hbm,...  2.46 us

profile of v4, /device:TPU:1, one launch (start us, length us, event | category | flops | bytes accessed | tf_op | source)
XLA Modules:
  0.0 53.2 jit_solution(1270813985677041552)
XLA Ops:
  0.6 50.1 %gate.1 = (f32[4,1,256]{2,1,0:T(1,128)}, f32[1,640,128]{2,1,0:T(8,128)}, f32[1,384,128]{2,1,0:T(8,128)}, f32[1,1]{1,0:T(1,128)}) custom-call(bf16[256,640]{1,0:T(8,128)(2,1)} %q_hbm.1, bf16[256,128]{1,0:T(8,128)(2,1)} %k_hbm.1, s32[4]{0:T(128)} %pos_hbm.1, bf16[1,640,128]{2,1,0:T(8,128)(2,1)} %wq_hbm.1, bf16[1,384,128]{2,1,0:T(8,128)(2,1)} %wk_hbm.1), custom_call_target="tpu_custom_call" | custom-call | tf_op jit(solution)/shard_map/gate/pallas_call | solution.py:488
  50.7 2.5 %place.1 = (f32[4,1,256]{2,1,0:T(1,128)}, f32[1,640,128]{2,1,0:T(8,128)}, f32[1,384,128]{2,1,0:T(8,128)}, f32[1,1]{1,0:T(1,128)}) custom-call(f32[4,1,256]{2,1,0:T(1,128)} %get-tuple-element.12.map_in, f32[1,640,128]{2,1,0:T(8,128)} %get-tuple-element.13.gq_in, f32[1,384,128]{2,1,0:T(8,128)} %get-tuple-element.14.gk_in, f32[1,1]{1,0:T(1,128)} %get-tuple-element.15.loss_in), custom_call_target="tpu_custom_call" | custom-call | tf_op jit(solution)/shard_map/place/pallas_call | solution.py:543
